TPU v7x, 256 devices: a whole 4x4x8 slice. The times are simulated.
256 devices in a mesh: tm: 64 (over z, y, x_lo), space: 4 (over x_hi, core).
Axes of the slice: x: 4 (x_hi: 2, x_lo: 2; x = x_hi * 2 + x_lo), y: 4, z: 8, core: 2. Of those that a mesh axis runs over, the one named last changes fastest.
Arguments:
- omega_hat: float32 [512, 256, 256], P('tm', 'space'), may hold values from -1 to 1, as said below
- delta_hat: float32 [512, 256, 256], P('tm', 'space'), may hold values from -1 to 1, as said below
Outputs:
- residual: float32 [512, 256, 256], P('tm', 'space')
- jvp: float32 [512, 256, 256], P('tm', 'space')
Inputs may be any that keep to these rules, and one draw needn't show every extreme that they name: `omega_hat`: coefficients of independent draws whose size falls with the wavenumbers. `delta_hat`: coefficients of independent draws whose size falls with the wavenumbers.
All inputs are finite; a program needn't handle non-finite values.
Results may differ from a plain program's by a relative error of at most 0.0003.
Values sent between devices are 32-bit elements; how exact they have to be, the bound alone decides.
A program may use at most 192 MiB of HBM per device.

v0:
```python
import math

import jax
import jax.numpy as jnp
from jax import lax
from jax.sharding import PartitionSpec as P

viscosity = 0.025
frequency = 0.3
forcing_wave = 4


def modes(n, offset, length):
    indices = offset + jnp.arange(length, dtype=jnp.int32)
    wavenum = jnp.where(indices == 1, n // 2, indices // 2)
    return (indices, wavenum)


def basis_matrix(n):
    points = jnp.arange(n, dtype=jnp.int32)
    indices, wavenum = modes(n, 0, n)
    angles = (points[:, None] * wavenum[None, :] % n).astype(jnp.float32) * (2.0 * math.pi / n)
    is_sine = (indices % 2 == 1) & (indices != 1)
    return jnp.where(is_sine[None, :], jnp.sin(angles), jnp.cos(angles))


def forward_matrix(n):
    indices, wavenum = modes(n, 0, n)
    weights = jnp.where(indices < 2, 1.0 / n, 2.0 / n).astype(jnp.float32)
    return basis_matrix(n).T * weights[:, None]


def derivative(values, axis_pos, offset, n):
    shape = values.shape
    length = shape[axis_pos]
    indices, wavenum = modes(n, offset, length)
    factor = jnp.where(indices >= 2, jnp.where(indices % 2 == 0, wavenum, -wavenum), 0).astype(
        jnp.float32
    )
    factor = factor.reshape((length,) + (1,) * (len(shape) - axis_pos - 1))
    paired = shape[:axis_pos] + (length // 2, 2) + shape[axis_pos + 1 :]
    swapped = jnp.flip(values.reshape(paired), axis_pos + 1).reshape(shape)
    return swapped * factor


def spectral_fields(omega, delta, kx_offset, n_x, n_y):
    indices_x, wave_x = modes(n_x, kx_offset, omega.shape[1])
    indices_y, wave_y = modes(n_y, 0, omega.shape[2])
    wave_x = wave_x.astype(jnp.float32)
    wave_y = wave_y.astype(jnp.float32)
    wave_sq = wave_x[:, None] * wave_x[:, None] + wave_y[None, :] * wave_y[None, :]
    inverse = jnp.where(wave_sq > 0, 1.0 / jnp.maximum(wave_sq, 1.0), 0.0)
    stream = omega * inverse
    stream_delta = delta * inverse
    stacked = jnp.stack(
        [
            derivative(stream, 2, 0, n_y),
            -derivative(stream, 1, kx_offset, n_x),
            derivative(omega, 1, kx_offset, n_x),
            derivative(omega, 2, 0, n_y),
            derivative(stream_delta, 2, 0, n_y),
            -derivative(stream_delta, 1, kx_offset, n_x),
            derivative(delta, 1, kx_offset, n_x),
            derivative(delta, 2, 0, n_y),
        ]
    )
    return (stacked, wave_sq)


def advect(physical):
    velocity_u, velocity_v, omega_dx, omega_dy = (
        physical[0],
        physical[1],
        physical[2],
        physical[3],
    )
    delta_u, delta_v, delta_dx, delta_dy = (physical[4], physical[5], physical[6], physical[7])
    advection = velocity_u * omega_dx + velocity_v * omega_dy
    linearized = (
        velocity_u * delta_dx + velocity_v * delta_dy + delta_u * omega_dx + delta_v * omega_dy
    )
    return jnp.stack([advection, linearized])


def assemble(omega, delta, nonlinear, wave_sq, kt_offset, kx_offset, n_t):
    idx_t = kt_offset + jnp.arange(omega.shape[0], dtype=jnp.int32)
    idx_x = kx_offset + jnp.arange(omega.shape[1], dtype=jnp.int32)
    idx_y = jnp.arange(omega.shape[2], dtype=jnp.int32)
    marked = (
        (idx_t == 0)[:, None, None]
        & (idx_x == 0)[None, :, None]
        & (idx_y == 2 * forcing_wave)[None, None, :]
    )
    forcing = jnp.where(marked, -float(forcing_wave), 0.0).astype(jnp.float32)
    residual = (
        frequency * derivative(omega, 0, kt_offset, n_t)
        + nonlinear[0]
        + viscosity * wave_sq * omega
        - forcing
    )
    tangent = (
        frequency * derivative(delta, 0, kt_offset, n_t)
        + nonlinear[1]
        + viscosity * wave_sq * delta
    )
    return (residual, tangent)


def time_synth(values, matrix):
    shape = values.shape
    merged = values.reshape(shape[0], shape[1], -1)
    result = jnp.einsum("fkm,tk->ftm", merged, matrix, precision=lax.Precision.HIGHEST)
    return result.reshape((shape[0], matrix.shape[0]) + shape[2:])


def per_device(omega_hat, delta_hat):
    nt_local, nx_local, n_y = omega_hat.shape
    n_t = nt_local * lax.axis_size("tm")
    n_x = nx_local * lax.axis_size("space")
    kt_offset = lax.axis_index("tm") * nt_local
    kx_offset = lax.axis_index("space") * nx_local
    highest = lax.Precision.HIGHEST
    fields, wave_sq = spectral_fields(omega_hat, delta_hat, kx_offset, n_x, n_y)
    along_y = jnp.einsum("ftxk,yk->ftxy", fields, basis_matrix(n_y), precision=highest)
    regrouped = lax.all_to_all(along_y, "space", split_axis=3, concat_axis=2, tiled=True)
    along_x = jnp.einsum("ftky,xk->ftxy", regrouped, basis_matrix(n_x), precision=highest)
    spread = lax.all_to_all(along_x, "tm", split_axis=2, concat_axis=1, tiled=True)
    physical = time_synth(spread, basis_matrix(n_t))
    products = advect(physical)
    spectra = time_synth(products, forward_matrix(n_t))
    returned = lax.all_to_all(spectra, "tm", split_axis=1, concat_axis=2, tiled=True)
    partial_value = jnp.einsum("ftxy,kx->ftky", returned, forward_matrix(n_x), precision=highest)
    gathered = lax.all_to_all(partial_value, "space", split_axis=2, concat_axis=3, tiled=True)
    nonlinear = jnp.einsum("ftxy,ky->ftxk", gathered, forward_matrix(n_y), precision=highest)
    return assemble(omega_hat, delta_hat, nonlinear, wave_sq, kt_offset, kx_offset, n_t)


def solution(mesh):
    in_specs = (P("tm", "space", None), P("tm", "space", None))
    out_specs = (P("tm", "space", None), P("tm", "space", None))
    return jax.shard_map(
        per_device, mesh=mesh, in_specs=in_specs, out_specs=out_specs, check_vma=False
    )
```

profile of v0, /device:TPU:1, one launch (start us, length us, event | category | flops | bytes accessed | tf_op | source)
XLA Modules:
  0.0 465.7 jit_solution(4226353925011990223)
XLA Ops:
  0.8 1.3 broadcast_multiply_fusion
  2.1 1.4 copy.25
  3.5 1.1 reshape.500
  4.6 1.1 reshape.502
  5.7 1.3 copy.27
  7.5 1.1 reshape.508
  8.6 1.1 reshape.510
  10.1 2.3 rev.34
  12.4 2.3 copy.26
  14.7 3.8 rev.35
  18.5 2.2 reshape.501
  20.7 3.6 rev.36
  24.3 2.2 reshape.503
  26.5 2.3 rev.37
  28.8 2.4 copy.28
  31.2 1.0 rev.38
  32.2 2.4 copy.30
  34.6 2.7 rev.39
  37.3 1.2 reshape.509
  38.4 2.7 rev.40
  41.1 1.2 reshape.511
  42.4 1.2 copy.32
  43.5 1.2 multiply_dynamic-update-slice_fusion.5
  44.8 1.2 negate_dynamic-update-slice_fusion.1
  45.9 1.2 multiply_dynamic-update-slice_fusion.4
  47.5 6.4 %fusion.69 = f32[8,8,64,256]{3,2,1,0:T(8,128)} fusion(f32[8,8,64,256]{3,2,1,0:T(8,128)S(1)} %multiply_dynamic-update-slice_fusion, s32[256]{0:T(256)S(1)} %fusion.87, pred[256]{0:T(512)(128)(4,1)S(1)} %compare_and_fusion), kind=kOutput, calls=%fused_computation.95 | convolution fusion | flops 3222208512 | bytes 8389888 | tf_op jit(solution)/shard_map/ftxk,yk->ftxy/dot_general | solution.py:124
  54.0 9.1 %copy.33 = f32[8,8,64,256]{2,1,0,3:T(8,128)} copy(f32[8,8,64,256]{3,2,1,0:T(8,128)} %fusion.69) | data formatting | bytes 8388608 | tf_op jit(solution)/shard_map/ftxk,yk->ftxy/dot_general | solution.py:124
  63.1 8.6 %reshape.522 = f32[4,1,262144]{2,1,0:T(1,128)} reshape(f32[256,8,8,64]{3,2,1,0:T(8,128)} %bitcast.96) | data formatting | bytes 8388608
  71.7 57.5 %all_to_all.69 = f32[4,1,262144]{2,1,0:T(1,128)} all-to-all(f32[4,1,262144]{2,1,0:T(1,128)} %reshape.522), channel_id=1, replica_groups=mesh['tm'=64,'space'=4] {'space'}, dimensions={0} | all-to-all | bytes 8388608 | tf_op jit(solution)/shard_map/all_to_all | solution.py:125
  129.3 0.6 broadcast.781
  129.9 15.5 %reduce = f32[4,262144]{1,0:T(4,128)} reduce(f32[4,1,262144]{2,1,0:T(1,128)} %all_to_all.69, f32[]{:T(128)} %broadcast.781), dimensions={1}, to_apply=%all_to_all.50.reduce_sub_computation | reduce | bytes 8388612 | tf_op jit(solution)/shard_map/all_to_all | solution.py:125
  145.4 9.3 %reshape.523 = f32[256,8,8,64]{3,2,1,0:T(8,128)} reshape(f32[4,262144]{1,0:T(4,128)} %reduce) | data formatting | bytes 8388608
  154.6 12.0 %copy.56 = f32[8,8,64,4,64]{2,3,4,1,0:T(4,128)} copy(f32[8,8,64,4,64]{2,1,0,4,3:T(8,128)} %bitcast.98) | data formatting | bytes 8388608 | tf_op jit(solution)/shard_map/all_to_all | solution.py:125
  166.6 8.9 %all_to_all.53 = f32[8,8,256,64]{2,3,1,0:T(8,128)} reshape(f32[8,8,4,64,64]{3,2,4,1,0:T(4,128)} %bitcast.99) | data formatting | bytes 8388608 | tf_op jit(solution)/shard_map/all_to_all | solution.py:125
  175.6 8.7 %convolution_bitcast_fusion = f32[8,8,256,64]{2,3,1,0:T(8,128)} fusion(f32[8,8,256,64]{2,3,1,0:T(8,128)} %all_to_all.53, s32[256]{0:T(256)S(1)} %fusion.87, pred[256]{0:T(512)(128)(4,1)S(1)} %compare_and_fusion), kind=kOutput, calls=%fused_computation.1 | convolution fusion | flops 3222208512 | bytes 8389888 | tf_op jit(solution)/shard_map/ftky,xk->ftxy/dot_general | solution.py:126
  184.2 9.1 %copy.35 = f32[8,8,256,64]{3,1,0,2:T(8,128)} copy(f32[8,8,256,64]{2,3,1,0:T(8,128)} %convolution_bitcast_fusion) | data formatting | bytes 8388608 | tf_op jit(solution)/shard_map/ftky,xk->ftxy/transpose | solution.py:126
  193.4 9.7 %reshape.524 = f32[64,1,16384]{2,1,0:T(1,128)} reshape(f32[256,8,8,64]{3,2,1,0:T(8,128)} %bitcast.97) | data formatting | bytes 8388608
  203.1 11.5 %all-to-all-start.1 = ((f32[64,1,16384]{2,1,0:T(1,128)}), f32[64,1,16384]{2,1,0:T(1,128)}, u32[]{:S(2)}, u32[]{:S(2)}) async-start(f32[64,1,16384]{2,1,0:T(1,128)} %reshape.524), calls=%async_computation.1 | async-start | bytes 8388608 | tf_op jit(solution)/shard_map/all_to_all | solution.py:127
  214.6 91.2 %all-to-all-done.1 = f32[64,1,16384]{2,1,0:T(1,128)} async-done(((f32[64,1,16384]{2,1,0:T(1,128)}), f32[64,1,16384]{2,1,0:T(1,128)}, u32[]{:S(2)}, u32[]{:S(2)}) %all-to-all-start.1) | async-done | bytes 4194336 | tf_op jit(solution)/shard_map/all_to_all | solution.py:127
  305.8 13.8 %reduce.1 = f32[64,16384]{1,0:T(8,128)} reduce(f32[64,1,16384]{2,1,0:T(1,128)} %all-to-all-done.1, f32[]{:T(128)} %broadcast.781), dimensions={1}, to_apply=%all_to_all.54.reduce_sub_computation | reduce | bytes 8388612 | tf_op jit(solution)/shard_map/all_to_all | solution.py:127
  319.6 7.4 %reshape.525 = f32[256,8,8,64]{3,2,1,0:T(8,128)} reshape(f32[64,16384]{1,0:T(8,128)} %reduce.1) | data formatting | bytes 8388608
  326.9 12.0 %copy.37 = f32[8,64,8,4,64]{4,3,2,1,0:T(4,128)} copy(f32[8,64,8,4,64]{4,2,0,3,1:T(8,128)} %bitcast.100) | data formatting | bytes 8388608 | tf_op jit(solution)/shard_map/all_to_all | solution.py:127
  338.9 8.7 %reshape.514 = f32[8,512,256]{2,1,0:T(8,128)} reshape(f32[8,64,8,4,64]{4,3,2,1,0:T(4,128)} %copy.37) | data formatting | bytes 8388608 | tf_op jit(solution)/shard_map/reshape | solution.py:111
  347.7 13.4 %convolution_bitcast_fusion.1 = f32[8,512,256]{2,1,0:T(8,128)S(1)} fusion(f32[8,512,256]{2,1,0:T(8,128)} %reshape.514, s32[512]{0:T(512)S(1)} %fusion.82, pred[512]{0:T(512)(128)(4,1)S(1)} %fusion.85), kind=kOutput, calls=%fused_computation.2 | convolution fusion | flops 6446383104 | bytes 8391168 | tf_op jit(solution)/shard_map/fkm,tk->ftm/dot_general | solution.py:112
  361.4 7.7 %fusion.11 = f32[512,2,256]{0,2,1:T(8,128)} fusion(f32[1,512,256]{2,1,0:T(8,128)S(1)} %get-tuple-element.3, f32[1,512,256]{2,1,0:T(8,128)S(1)} %get-tuple-element.2, f32[512]{0:T(512)S(1)} %fusion.88, s32[512]{0:T(512)S(1)} %fusion.82, pred[512]{0:T(512)(128)(4,1)S(1)} %fusion.85), kind=kOutput, calls=%fused_computation.20 | convolution fusion | flops 1615069184 | bytes 2101760 | tf_op jit(solution)/shard_map/fkm,tk->ftm/dot_general | solution.py:112
  369.1 2.1 copy.39
  371.2 2.9 reshape.526
  374.0 8.9 %all-to-all-start.2 = ((f32[64,1,4096]{2,1,0:T(1,128)}), f32[64,1,4096]{2,1,0:T(1,128)S(1)}, u32[]{:S(2)}, u32[]{:S(2)}) async-start(f32[64,1,4096]{2,1,0:T(1,128)} %reshape.526), calls=%async_computation.2 | async-start | bytes 2097152 | tf_op jit(solution)/shard_map/all_to_all | solution.py:131
  383.0 24.5 %all-to-all-done.2 = f32[64,1,4096]{2,1,0:T(1,128)S(1)} async-done(((f32[64,1,4096]{2,1,0:T(1,128)}), f32[64,1,4096]{2,1,0:T(1,128)S(1)}, u32[]{:S(2)}, u32[]{:S(2)}) %all-to-all-start.2) | async-done | bytes 1048608 | tf_op jit(solution)/shard_map/all_to_all | solution.py:131
  407.5 4.5 reduce.2
  412.0 2.6 reshape.527
  415.3 5.5 %fusion.2 = f32[2,8,256,64]{2,3,1,0:T(8,128)} fusion(f32[2,8,256,64]{3,1,2,0:T(8,128)S(1)} %bitcast.107, f32[256]{0:T(256)S(1)} %compare_select_fusion.5, s32[256]{0:T(256)S(1)} %fusion.87, pred[256]{0:T(512)(128)(4,1)S(1)} %compare_and_fusion), kind=kOutput, calls=%fused_computation.13 | convolution fusion | flops 806354944 | bytes 2099456 | tf_op jit(solution)/shard_map/ftxy,kx->ftky/dot_general | solution.py:132
  420.8 2.5 copy.43
  423.3 2.4 reshape.528
  425.7 9.1 %all-to-all-start.3 = ((f32[4,1,65536]{2,1,0:T(1,128)}), f32[4,1,65536]{2,1,0:T(1,128)S(1)}, u32[]{:S(2)}, u32[]{:S(2)}) async-start(f32[4,1,65536]{2,1,0:T(1,128)} %reshape.528), calls=%async_computation.3 | async-start | bytes 2097152 | tf_op jit(solution)/shard_map/all_to_all | solution.py:133
  434.8 0.8 rev.33
  435.7 0.8 rev.42
  436.6 13.2 %all-to-all-done.3 = f32[4,1,65536]{2,1,0:T(1,128)S(1)} async-done(((f32[4,1,65536]{2,1,0:T(1,128)}), f32[4,1,65536]{2,1,0:T(1,128)S(1)}, u32[]{:S(2)}, u32[]{:S(2)}) %all-to-all-start.3) | async-done | bytes 1048608 | tf_op jit(solution)/shard_map/all_to_all | solution.py:133
  449.9 4.7 %reduce.3 = f32[4,65536]{1,0:T(4,128)} reduce(f32[4,1,65536]{2,1,0:T(1,128)S(1)} %all-to-all-done.3, f32[]{:T(128)} %broadcast.781), dimensions={1}, to_apply=%all_to_all.61.reduce_sub_computation | reduce | bytes 2097156 | tf_op jit(solution)/shard_map/all_to_all | solution.py:133
  454.6 2.2 reshape.529
  456.8 2.7 copy.57
  459.5 2.6 all_to_all.64
  462.1 2.1 fusion.65
  464.2 1.2 fusion.37
  (45 shorter events, 2.5 us)
Async XLA Ops:
  0.6 4.0 copy-start.1
  2.1 6.4 %copy-start = (f32[8,64,256]{2,1,0:T(8,128)S(1)}, f32[8,64,256]{2,1,0:T(8,128)}, u32[]{:S(2)}) copy-start(f32[8,64,256]{2,1,0:T(8,128)} %param.3) | copy-start | bytes 1572868
  42.4 4.7 %copy-start.2 = (f32[1,8,64,256]{3,2,1,0:T(8,128)S(1)}, f32[1,8,64,256]{3,2,1,0:T(8,128)}, u32[]{:S(2)}) copy-start(f32[1,8,64,256]{3,2,1,0:T(8,128)} %copy.28) | copy-start | bytes 1572868
  42.4 4.8 %copy-start.3 = (f32[1,8,64,256]{3,2,1,0:T(8,128)S(1)}, f32[1,8,64,256]{3,2,1,0:T(8,128)}, u32[]{:S(2)}) copy-start(f32[1,8,64,256]{3,2,1,0:T(8,128)} %copy.30) | copy-start | bytes 1572868
  43.5 3.6 copy-start.5
  43.5 3.8 copy-start.6
  43.5 3.9 copy-start.4
  203.1 102.7 %all-to-all-start.1 = ((f32[64,1,16384]{2,1,0:T(1,128)}), f32[64,1,16384]{2,1,0:T(1,128)}, u32[]{:S(2)}, u32[]{:S(2)}) async-start(f32[64,1,16384]{2,1,0:T(1,128)} %reshape.524), calls=%async_computation.1 | async-start | bytes 8388608 | tf_op jit(solution)/shard_map/all_to_all | solution.py:127
  374.0 33.4 %all-to-all-start.2 = ((f32[64,1,4096]{2,1,0:T(1,128)}), f32[64,1,4096]{2,1,0:T(1,128)S(1)}, u32[]{:S(2)}, u32[]{:S(2)}) async-start(f32[64,1,4096]{2,1,0:T(1,128)} %reshape.526), calls=%async_computation.2 | async-start | bytes 2097152 | tf_op jit(solution)/shard_map/all_to_all | solution.py:131
  425.7 24.2 %all-to-all-start.3 = ((f32[4,1,65536]{2,1,0:T(1,128)}), f32[4,1,65536]{2,1,0:T(1,128)S(1)}, u32[]{:S(2)}, u32[]{:S(2)}) async-start(f32[4,1,65536]{2,1,0:T(1,128)} %reshape.528), calls=%async_computation.3 | async-start | bytes 2097152 | tf_op jit(solution)/shard_map/all_to_all | solution.py:133
  459.5 4.7 %copy-start.7 = (f32[4,2,64,256]{3,2,1,0:T(8,128)S(1)}, f32[4,2,64,256]{3,2,1,0:T(8,128)}, u32[]{:S(2)}) copy-start(f32[4,2,64,256]{3,2,1,0:T(8,128)} %rev.33) | copy-start | bytes 1572868
  459.5 4.7 %copy-start.8 = (f32[4,2,64,256]{3,2,1,0:T(8,128)S(1)}, f32[4,2,64,256]{3,2,1,0:T(8,128)}, u32[]{:S(2)}) copy-start(f32[4,2,64,256]{3,2,1,0:T(8,128)} %rev.42) | copy-start | bytes 1572868
where the time goes:
time: 471 us; the launch traced here: 466 us
  local copies, waits for them, and re-layouts  159 us (34%)
  waiting for transfers between devices  129 us (27%)
  blocking collectives  57.5 us (12%)
  other arithmetic  45.3 us (10%)
  matrix products  43.8 us (9%)
  starting transfers between devices  29.5 us (6%)
    all_to_all x1, waiting for transfers between devices, per_device(): lax.all_to_all(along_x, 'tm', split_axis=2, concat_axis=1, tiled=True)  91.2 us
    all_to_all x1, blocking collectives, per_device(): lax.all_to_all(along_y, 'space', split_axis=3, concat_axis=2, tiled=True)  57.5 us
    unnamed x28, local copies, waits for them, and re-layouts  46.9 us
    all_to_all x1, waiting for transfers between devices, per_device(): lax.all_to_all(spectra, 'tm', split_axis=1, concat_axis=2, tiled=True)  24.5 us
    all_to_all x3, local copies, waits for them, and re-layouts, per_device(): lax.all_to_all(along_y, 'space', split_axis=3, concat_axis=2, tiled=True)  21.5 us
    dot_general x2, matrix products, time_synth(): jnp.einsum('fkm,tk->ftm', merged, matrix, precision=lax.Precision.HIGHEST)  21.1 us
    rev x10, local copies, waits for them, and re-layouts, derivative(): swapped = jnp.flip(values.reshape(paired), axis_pos + 1).reshape(shape)  20.2 us
    reshape x12, local copies, waits for them, and re-layouts, derivative(): swapped = jnp.flip(values.reshape(paired), axis_pos + 1).reshape(shape)  19.3 us
  transfers between devices with their start and end apart: 3, of which 3 were waited for; matrix products, arithmetic and copies ran while one was open for 0% of the time, Pallas kernels for 0%

commit v1 on v0

v1 whole, which is shorter than its diff:
```python
import functools

import jax
import jax.numpy as jnp
import ml_dtypes
import numpy as np
from jax import lax
from jax.experimental import pallas as pl
from jax.experimental.pallas import tpu as pltpu
from jax.sharding import PartitionSpec as P

MESH = pl.DeviceIdType.MESH
viscosity = 0.025
frequency = 0.3
forcing_wave = 4

NT, NX, NY = 512, 256, 256
GROUP = 2
OUTER = 256 // GROUP
ROWS = 4 * GROUP
SPAN = NT // GROUP


def wavenumbers(n):
    indices = np.arange(n)
    return np.where(indices == 1, n // 2, indices // 2)


def basis_matrix(n):
    points, indices, wave = np.arange(n), np.arange(n), wavenumbers(n)
    angles = (points[:, None] * wave[None, :] % n) * (2.0 * np.pi / n)
    is_sine = (indices % 2 == 1) & (indices != 1)
    return np.where(is_sine[None, :], np.sin(angles), np.cos(angles))


def forward_matrix(n):
    weights = np.where(np.arange(n) < 2, 1.0 / n, 2.0 / n)
    return basis_matrix(n).T * weights[:, None]


def derivative_matrix(n):
    wave = wavenumbers(n)
    out = np.zeros((n, n))
    for j in range(2, n):
        if j % 2 == 0:
            out[j, j + 1] = wave[j]
        else:
            out[j, j - 1] = -wave[j]
    return out


def split_constant(matrix):
    high = matrix.astype(np.float32).astype(ml_dtypes.bfloat16)
    low = (matrix - high.astype(np.float64)).astype(np.float32).astype(ml_dtypes.bfloat16)
    return [high, low]


def x_order():
    core, x_hi, tm = np.meshgrid(np.arange(2), np.arange(2), np.arange(64), indexing="ij")
    return (128 * x_hi + 64 * core + tm).reshape(-1)


def constants():
    order = x_order()
    synth_t, forward_t = basis_matrix(NT), forward_matrix(NT)
    synth_x, synth_y = basis_matrix(NX), basis_matrix(NY)
    slope_x = (synth_x @ derivative_matrix(NX))[:, order]
    slope_y = synth_y @ derivative_matrix(NY)
    time = np.stack(split_constant(synth_t) + split_constant(forward_t))
    space = np.stack(
        split_constant(synth_x[:, order])
        + split_constant(slope_x)
        + split_constant(synth_y.T)
        + split_constant(slope_y.T)
        + split_constant(forward_matrix(NX)[order])
        + split_constant(forward_matrix(NY).T)
    )
    wave_x, wave_y = wavenumbers(NX)[order], wavenumbers(NY)
    square = (wave_x[:, None] ** 2 + wave_y[None, :] ** 2).astype(np.float64)
    inverse = np.where(square > 0, 1.0 / np.maximum(square, 1.0), 0.0).astype(np.float32)
    return time, space, inverse


def halves(value):
    high = value.astype(jnp.bfloat16)
    return high, (value - high.astype(jnp.float32)).astype(jnp.bfloat16)


def product(left, right):
    dot = functools.partial(jnp.dot, preferred_element_type=jnp.float32)
    return dot(left[0], right[0]) + (dot(left[1], right[0]) + dot(left[0], right[1]))


def both(ref, *index):
    return jnp.concatenate([ref[(*index, h)] for h in range(2)], axis=1)


def kernel(
    omega_ref,
    delta_ref,
    time_hbm,
    space_hbm,
    inverse_hbm,
    residual_ref,
    jvp_ref,
    time_ref,
    space_ref,
    inverse_ref,
    a_src,
    a_dst,
    c1_src,
    c1_dst,
    c2_src,
    c2_dst,
    fields,
    r2_src,
    r2_dst,
    r1_src,
    r1_dst,
    b_src,
    b_dst,
    linear,
    const_sem,
    send_sem,
    recv_sem,
):
    tm, space = lax.axis_index("tm"), lax.axis_index("space")
    z, y, x_lo, x_hi, core = tm // 8, (tm // 2) % 4, tm % 2, space // 2, space % 2
    outer = x_hi * 64 + tm
    inputs = (omega_ref, delta_ref)

    loads = [
        pltpu.make_async_copy(src, dst, const_sem.at[k])
        for k, (src, dst) in enumerate(
            ((time_hbm, time_ref), (space_hbm, space_ref), (inverse_hbm, inverse_ref))
        )
    ]
    for load in loads:
        load.start()

    def tm_partner(step):
        dz, dy, dx = (3 * step) % 8, (step // 8) % 4, step // 32
        return ((z + dz) % 8) * 8 + ((y + dy) % 4) * 2 + (x_lo + dx) % 2

    def outer_partner(step):
        dz, dy, dx = (3 * step) % 8, (step // 8) % 4, step // 32
        x = (x_hi * 2 + x_lo + dx) % 4
        return ((z + dz) % 8) * 8 + ((y + dy) % 4) * 2 + x % 2, x // 2

    def settle(buffer, sem):
        pltpu.make_async_copy(buffer, buffer, sem).wait()

    def rows8(index):
        return pl.ds(pl.multiple_of(index * 8, 8), 8)

    def exchange_tm(stage, a, src, dst):
        send, recv = send_sem.at[stage, a], recv_sem.at[stage, a]
        pltpu.make_async_copy(src.at[a, :, rows8(tm)], dst.at[a, :, rows8(tm)], recv).start()

        def body(step, carry):
            partner = tm_partner(step)
            pltpu.make_async_remote_copy(
                src_ref=src.at[a, :, rows8(partner)],
                dst_ref=dst.at[a, :, rows8(tm)],
                send_sem=send,
                recv_sem=recv,
                device_id=(partner, space),
                device_id_type=MESH,
            ).start()
            return carry

        lax.fori_loop(1, 64, body, 0)

    def message(index):
        return pl.ds(pl.multiple_of(index * ROWS, ROWS), ROWS)

    def exchange_outer(stage, a, src, dst):
        send, recv = send_sem.at[stage, a], recv_sem.at[stage, a]
        pltpu.make_async_copy(src.at[a, message(outer)], dst.at[a, message(outer)], recv).start()

        def body(step, carry):
            partner, partner_hi = outer_partner(step)
            pltpu.make_async_remote_copy(
                src_ref=src.at[a, message(partner_hi * 64 + partner)],
                dst_ref=dst.at[a, message(outer)],
                send_sem=send,
                recv_sem=recv,
                device_id=(partner, partner_hi * 2 + core),
                device_id_type=MESH,
            ).start()
            return carry

        lax.fori_loop(1, OUTER, body, 0)

    def span(index):
        return pl.ds(pl.multiple_of(index * SPAN, SPAN), SPAN)

    sibling = (tm, x_hi * 2 + (1 - core))

    def gather_group(a):
        send, recv = send_sem.at[1, a], recv_sem.at[1, a]
        pltpu.make_async_copy(c1_src.at[a, :, span(core)], c1_dst.at[a, core], recv).start()
        pltpu.make_async_remote_copy(
            src_ref=c1_src.at[a, :, span(1 - core)],
            dst_ref=c1_dst.at[a, core],
            send_sem=send,
            recv_sem=recv,
            device_id=sibling,
            device_id_type=MESH,
        ).start()

    def scatter_group(a):
        send, recv = send_sem.at[4, a], recv_sem.at[4, a]
        pltpu.make_async_copy(r1_src.at[a, core], r1_dst.at[a, :, span(core)], recv).start()
        pltpu.make_async_remote_copy(
            src_ref=r1_src.at[a, 1 - core],
            dst_ref=r1_dst.at[a, :, span(core)],
            send_sem=send,
            recv_sem=recv,
            device_id=sibling,
            device_id_type=MESH,
        ).start()

    def time_transform(which, value):
        matrix = (time_ref[which], time_ref[which + 1])
        return product(matrix, halves(value))

    def lane_row(half, point, member):
        return pl.ds((half * 2 + point) * GROUP + member, OUTER, stride=ROWS)

    for a in range(2):
        for r in range(8):
            for h in range(2):
                a_src[a, h, pl.ds(r, 64, stride=8), :] = inputs[a][r, :, h * 128 : h * 128 + 128]
        exchange_tm(0, a, a_src, a_dst)

    row = lax.broadcasted_iota(jnp.int32, (64, NY), 0) + space * 64
    col = lax.broadcasted_iota(jnp.int32, (64, NY), 1)
    wave_x = jnp.where(row == 1, NX // 2, row // 2).astype(jnp.float32)
    wave_y = jnp.where(col == 1, NY // 2, col // 2).astype(jnp.float32)
    damping = viscosity * (wave_x * wave_x + wave_y * wave_y)
    forced = (row == 0) & (col == 2 * forcing_wave)
    for a in range(2):
        for r in range(8):
            wave_t = (tm * 4 + r // 2).astype(jnp.float32)
            rate = frequency * wave_t if r % 2 == 0 else -frequency * wave_t
            term = rate * inputs[a][r ^ 1] + damping * inputs[a][r]
            if a == 0 and r == 0:
                force = jnp.where(tm == 0, -float(forcing_wave), 0.0).astype(jnp.float32)
                term = term - jnp.where(forced, force, 0.0)
            linear[a, r] = term

    for load in loads:
        load.wait()

    for a in range(2):
        settle(a_dst.at[a], recv_sem.at[0, a])
        value = time_transform(0, both(a_dst, a))
        for h in range(2):
            c1_src[a, h] = value[:, h * 128 : h * 128 + 128]
        gather_group(a)
        settle(c1_dst.at[a], recv_sem.at[1, a])
        for g in range(GROUP):
            for h in range(2):
                for t in range(2):
                    c2_src[a, lane_row(h, t, g), :] = c1_dst[a, g, h, t * OUTER : (t + 1) * OUTER, :]
        exchange_outer(2, a, c2_src, c2_dst)

    for a in range(2):
        settle(c2_dst.at[a], recv_sem.at[2, a])
        planes = []
        for t in range(2):
            columns = [
                jnp.concatenate([c2_dst[a, lane_row(h, t, g), :] for g in range(GROUP)], axis=0)
                for h in range(2)
            ]
            planes.append(jnp.concatenate(columns, axis=1))
        inverse = inverse_ref[...]
        right = halves(jnp.concatenate([inverse * planes[0], inverse * planes[1]] + planes, axis=1))
        for k, (along_x, along_y) in enumerate(((0, 6), (2, 4))):
            mixed = product((space_ref[along_x], space_ref[along_x + 1]), right)
            stacked = jnp.concatenate([mixed[:, q * 256 : q * 256 + 256] for q in range(4)], axis=0)
            grid = product(halves(stacked), (space_ref[along_y], space_ref[along_y + 1]))
            for q in range(4):
                fields[a, k, q] = grid[q * 256 : q * 256 + 256]
        points = []
        for t in range(2):
            total = fields[0, 0, t] * fields[a, 1, 2 + t] - fields[0, 1, t] * fields[a, 0, 2 + t]
            if a == 1:
                total = total + (
                    fields[1, 0, t] * fields[0, 1, 2 + t] - fields[1, 1, t] * fields[0, 0, 2 + t]
                )
            points.append(total)
        mixed = product((space_ref[8], space_ref[9]), halves(jnp.concatenate(points, axis=1)))
        stacked = jnp.concatenate([mixed[:, :256], mixed[:, 256:]], axis=0)
        modes = product(halves(stacked), (space_ref[10], space_ref[11]))
        for t in range(2):
            for g in range(GROUP):
                for h in range(2):
                    start = t * 256 + g * OUTER
                    r2_src[a, lane_row(h, t, g), :] = modes[
                        start : start + OUTER, h * 128 : h * 128 + 128
                    ]
        exchange_outer(3, a, r2_src, r2_dst)

    for a in range(2):
        settle(r2_dst.at[a], recv_sem.at[3, a])
        for g in range(GROUP):
            for h in range(2):
                for t in range(2):
                    r1_src[a, g, h, t * OUTER : (t + 1) * OUTER, :] = r2_dst[a, lane_row(h, t, g), :]
        scatter_group(a)
        settle(r1_dst.at[a], recv_sem.at[4, a])
        value = time_transform(2, both(r1_dst, a))
        for h in range(2):
            b_src[a, h] = value[:, h * 128 : h * 128 + 128]
        exchange_tm(5, a, b_src, b_dst)

    outputs = (residual_ref, jvp_ref)
    for a in range(2):
        settle(b_dst.at[a], recv_sem.at[5, a])
        for r in range(8):
            for h in range(2):
                lanes = slice(h * 128, h * 128 + 128)
                outputs[a][r, :, lanes] = linear[a, r, :, lanes] + b_dst[a, h, pl.ds(r, 64, stride=8), :]

    for a in range(2):
        settle(a_src.at[a, :, pl.ds(0, NT - 8)], send_sem.at[0, a])
        settle(c1_src.at[a, :, pl.ds(0, SPAN)], send_sem.at[1, a])
        settle(c2_src.at[a, pl.ds(0, 1024 - ROWS)], send_sem.at[2, a])
        settle(r2_src.at[a, pl.ds(0, 1024 - ROWS)], send_sem.at[3, a])
        settle(r1_src.at[a, 0], send_sem.at[4, a])
        settle(b_src.at[a, :, pl.ds(0, NT - 8)], send_sem.at[5, a])


def solution(mesh):
    time, space, inverse = constants()

    def per_device(omega, delta):
        block = jax.ShapeDtypeStruct(omega.shape, jnp.float32)
        vmem, anywhere = pl.BlockSpec(memory_space=pltpu.VMEM), pl.BlockSpec(memory_space=pl.ANY)
        strips = pltpu.VMEM((2, 2, NT, 128), jnp.float32)
        pieces = pltpu.VMEM((2, GROUP, 2, SPAN, 128), jnp.float32)
        tiles = pltpu.VMEM((2, OUTER * ROWS, 128), jnp.float32)
        return pl.pallas_call(
            kernel,
            out_shape=(block, block),
            in_specs=[vmem, vmem, anywhere, anywhere, anywhere],
            out_specs=(vmem, vmem),
            scratch_shapes=[
                pltpu.VMEM(time.shape, jnp.bfloat16),
                pltpu.VMEM(space.shape, jnp.bfloat16),
                pltpu.VMEM(inverse.shape, jnp.float32),
                strips,
                strips,
                strips,
                pieces,
                tiles,
                tiles,
                pltpu.VMEM((2, 2, 4, NX, NY), jnp.float32),
                tiles,
                tiles,
                pieces,
                strips,
                strips,
                strips,
                pltpu.VMEM((2, 8, 64, NY), jnp.float32),
                pltpu.SemaphoreType.DMA((3,)),
                pltpu.SemaphoreType.DMA((6, 2)),
                pltpu.SemaphoreType.DMA((6, 2)),
            ],
            compiler_params=pltpu.CompilerParams(
                has_side_effects=True, vmem_limit_bytes=58 * 1024 * 1024
            ),
        )(omega, delta, time, space, inverse)

    specs = (P("tm", "space", None), P("tm", "space", None))
    return jax.shard_map(per_device, mesh=mesh, in_specs=specs, out_specs=specs, check_vma=False)
```

time: 471 us -> 120 us (0.25); the launches traced: 466 us -> 119 us
  local copies, waits for them, and re-layouts: 159 us -> 3.74 us
  waiting for transfers between devices: 129 us -> 0 us
  Pallas kernels: 0 us -> 115 us
  blocking collectives: 57.5 us -> 0 us
  other arithmetic: 45.3 us -> 0 us
  matrix products: 43.8 us -> 0 us
  starting transfers between devices: 29.5 us -> 0 us
    all_to_all x3 -> x0, waiting for transfers between devices: 129 us -> none  [the longest x1 91.2 us: per_device(): lax.all_to_all(along_x, 'tm', split_axis=2, concat_axis=1, tiled=True)]
    pallas_call x0 -> x1, Pallas kernels: none -> 115 us  [per_device(): pl.pallas_call(kernel, out_shape=(block, block), in_specs=[vmem, vmem, an...]
    all_to_all x1 -> x0, blocking collectives: 57.5 us -> none  [per_device(): lax.all_to_all(along_y, 'space', split_axis=3, concat_axis=2, tiled=True)]
    dot_general x6 -> x0, matrix products: 43.8 us -> none  [the longest x2 21.1 us: time_synth(): jnp.einsum('fkm,tk->ftm', merged, matrix, precision=lax.Precision.HIGHEST)]
    unnamed x28 -> x2, local copies, waits for them, and re-layouts: 46.9 us -> 3.74 us
    all_to_all x8 -> x0, local copies, waits for them, and re-layouts: 39.5 us -> none  [the longest x3 21.5 us: per_device(): lax.all_to_all(along_y, 'space', split_axis=3, concat_axis=2, tiled=True)]
    all_to_all x4 -> x0, other arithmetic: 38.4 us -> none  [the longest x1 15.5 us: per_device(): lax.all_to_all(along_y, 'space', split_axis=3, concat_axis=2, tiled=True)]
    reshape x14 -> x0, local copies, waits for them, and re-layouts: 30.1 us -> none  [the longest x12 19.3 us: derivative(): swapped = jnp.flip(values.reshape(paired), axis_pos + 1).reshape(shape)]
  transfers between devices with their start and end apart: 3 -> 0, of which waited for: 3 -> 0; matrix products, arithmetic and copies ran while one was open for 0% -> 0% of each run, Pallas kernels for 0% -> 0%
where the time goes in v1:
time: 120 us; the launch traced here: 119 us
  Pallas kernels  115 us (96%)
  local copies, waits for them, and re-layouts  3.74 us (3%)
    pallas_call x1, Pallas kernels, per_device(): pl.pallas_call(kernel, out_shape=(block, block), in_specs=[vmem, vmem, an...  115 us
    unnamed x2, local copies, waits for them, and re-layouts  3.74 us

profile of v1, /device:TPU:1, one launch (start us, length us, event | category | flops | bytes accessed | tf_op | source)
XLA Modules:
  0.0 119.4 jit_solution(13807414760141494556)
XLA Ops:
  0.6 115.0 %shard_map.68 = (f32[8,64,256]{2,1,0:T(8,128)}, f32[8,64,256]{2,1,0:T(8,128)}) custom-call(f32[8,64,256]{2,1,0:T(8,128)} %omega_ref.1, f32[8,64,256]{2,1,0:T(8,128)} %delta_ref.1, bf16[4,512,512]{2,1,0:T(8,128)(2,1)} %constant.6.clone.time_hbm, bf16[12,256,256]{2,1,0:T(8,128)(2,1)} %constant.7.clone.space_hbm, f32[256,256]{1,0:T(8,128)} %constant.8.clone.inverse_hbm), custom_call_target="tpu_custom_call" | custom-call | tf_op jit(solution)/shard_map/pallas_call | solution.py:345
  115.7 1.9 %copy.9 = f32[8,64,256]{2,1,0:T(8,128)} copy(f32[8,64,256]{2,1,0:T(8,128)} %get-tuple-element.4) | data formatting | bytes 1048576
  117.5 1.9 %copy.10 = f32[8,64,256]{2,1,0:T(8,128)} copy(f32[8,64,256]{2,1,0:T(8,128)} %get-tuple-element.5) | data formatting | bytes 1048576

commit v2 on v1

--- a/solution.py
+++ b/solution.py
@@ -96,13 +96,15 @@
 
 
 def kernel(
-    omega_ref,
-    delta_ref,
+    omega_hbm,
+    delta_hbm,
     time_hbm,
     space_hbm,
     inverse_hbm,
     residual_ref,
     jvp_ref,
+    omega_ref,
+    delta_ref,
     time_ref,
     space_ref,
     inverse_ref,
@@ -123,6 +125,7 @@
     const_sem,
     send_sem,
     recv_sem,
+    plane_sem,
 ):
     tm, space = lax.axis_index("tm"), lax.axis_index("space")
     z, y, x_lo, x_hi, core = tm // 8, (tm // 2) % 4, tm % 2, space // 2, space % 2
@@ -132,20 +135,44 @@
     loads = [
         pltpu.make_async_copy(src, dst, const_sem.at[k])
         for k, (src, dst) in enumerate(
-            ((time_hbm, time_ref), (space_hbm, space_ref), (inverse_hbm, inverse_ref))
+            (
+                (omega_hbm, omega_ref),
+                (delta_hbm, delta_ref),
+                (time_hbm, time_ref),
+                (space_hbm, space_ref),
+                (inverse_hbm, inverse_ref),
+            )
         )
     ]
+
+    barrier = pltpu.get_barrier_semaphore()
+    column = [(((z + dz) % 8) * 8 + y * 2 + x_lo, space) for dz in range(1, 8)]
+    greeted = column + [(tm, x_hi * 2 + (1 - core))]
+    for dy in range(4):
+        for dx in range(4):
+            if dy or dx:
+                x = (x_hi * 2 + x_lo + dx) % 4
+                greeted.append((z * 8 + ((y + dy) % 4) * 2 + x % 2, (x // 2) * 2 + core))
+    for device in greeted:
+        pl.semaphore_signal(barrier, inc=1, device_id=device, device_id_type=MESH)
     for load in loads:
         load.start()
 
+    def far_first(step, plane):
+        later = step - plane
+        level = later // (2 * plane)
+        distance = jnp.where(step < plane, 4, (3 - level) * (1 - 2 * (later % 2)))
+        place = jnp.where(step < plane, step, (later % (2 * plane)) // 2)
+        return distance, jnp.where(level < 3, place, later - 6 * plane + 1)
+
     def tm_partner(step):
-        dz, dy, dx = (3 * step) % 8, (step // 8) % 4, step // 32
-        return ((z + dz) % 8) * 8 + ((y + dy) % 4) * 2 + (x_lo + dx) % 2
+        dz, place = far_first(step, 8)
+        return ((z + dz + 8) % 8) * 8 + ((y + place // 2) % 4) * 2 + (x_lo + place) % 2
 
     def outer_partner(step):
-        dz, dy, dx = (3 * step) % 8, (step // 8) % 4, step // 32
-        x = (x_hi * 2 + x_lo + dx) % 4
-        return ((z + dz) % 8) * 8 + ((y + dy) % 4) * 2 + x % 2, x // 2
+        dz, place = far_first(step, 16)
+        x = (x_hi * 2 + x_lo + place) % 4
+        return ((z + dz + 8) % 8) * 8 + ((y + place // 4) % 4) * 2 + x % 2, x // 2
 
     def settle(buffer, sem):
         pltpu.make_async_copy(buffer, buffer, sem).wait()
@@ -169,7 +196,7 @@
             ).start()
             return carry
 
-        lax.fori_loop(1, 64, body, 0)
+        lax.fori_loop(0, 63, body, 0)
 
     def message(index):
         return pl.ds(pl.multiple_of(index * ROWS, ROWS), ROWS)
@@ -190,7 +217,7 @@
             ).start()
             return carry
 
-        lax.fori_loop(1, OUTER, body, 0)
+        lax.fori_loop(0, OUTER - 1, body, 0)
 
     def span(index):
         return pl.ds(pl.multiple_of(index * SPAN, SPAN), SPAN)
@@ -229,9 +256,15 @@
         return pl.ds((half * 2 + point) * GROUP + member, OUTER, stride=ROWS)
 
     for a in range(2):
+        loads[a].wait()
         for r in range(8):
             for h in range(2):
                 a_src[a, h, pl.ds(r, 64, stride=8), :] = inputs[a][r, :, h * 128 : h * 128 + 128]
+    pl.semaphore_wait(barrier, len(greeted))
+    for device in column:
+        pl.semaphore_signal(plane_sem, inc=1, device_id=device, device_id_type=MESH)
+    pl.semaphore_wait(plane_sem, len(column))
+    for a in range(2):
         exchange_tm(0, a, a_src, a_dst)
 
     row = lax.broadcasted_iota(jnp.int32, (64, NY), 0) + space * 64
@@ -250,7 +283,7 @@
                 term = term - jnp.where(forced, force, 0.0)
             linear[a, r] = term
 
-    for load in loads:
+    for load in loads[2:]:
         load.wait()
 
     for a in range(2):
@@ -333,21 +366,42 @@
         settle(b_src.at[a, :, pl.ds(0, NT - 8)], send_sem.at[5, a])
 
 
+PARTS = 2
+
+
+def hand_over(residual_in, jvp_in, residual_ref, jvp_ref, one, two, sem, out_sem):
+    copies, outs = [], []
+    for a, (src, mid, dst) in enumerate(((residual_in, one, residual_ref), (jvp_in, two, jvp_ref))):
+        for k in range(PARTS):
+            part = pl.ds(k * (8 // PARTS), 8 // PARTS)
+            copies.append(pltpu.make_async_copy(src.at[part], mid.at[part], sem.at[a, k]))
+            outs.append(pltpu.make_async_copy(mid.at[part], dst.at[part], out_sem.at[a, k]))
+    for copy in copies:
+        copy.start()
+    for copy, out in zip(copies, outs):
+        copy.wait()
+        out.start()
+    for out in outs:
+        out.wait()
+
+
 def solution(mesh):
     time, space, inverse = constants()
 
     def per_device(omega, delta):
         block = jax.ShapeDtypeStruct(omega.shape, jnp.float32)
-        vmem, anywhere = pl.BlockSpec(memory_space=pltpu.VMEM), pl.BlockSpec(memory_space=pl.ANY)
+        vmem, main = pl.BlockSpec(memory_space=pltpu.VMEM), pl.BlockSpec(memory_space=pltpu.HBM)
         strips = pltpu.VMEM((2, 2, NT, 128), jnp.float32)
         pieces = pltpu.VMEM((2, GROUP, 2, SPAN, 128), jnp.float32)
         tiles = pltpu.VMEM((2, OUTER * ROWS, 128), jnp.float32)
-        return pl.pallas_call(
+        results = pl.pallas_call(
             kernel,
             out_shape=(block, block),
-            in_specs=[vmem, vmem, anywhere, anywhere, anywhere],
+            in_specs=[main] * 5,
             out_specs=(vmem, vmem),
             scratch_shapes=[
+                pltpu.VMEM(block.shape, jnp.float32),
+                pltpu.VMEM(block.shape, jnp.float32),
                 pltpu.VMEM(time.shape, jnp.bfloat16),
                 pltpu.VMEM(space.shape, jnp.bfloat16),
                 pltpu.VMEM(inverse.shape, jnp.float32),
@@ -365,14 +419,23 @@
                 strips,
                 strips,
                 pltpu.VMEM((2, 8, 64, NY), jnp.float32),
-                pltpu.SemaphoreType.DMA((3,)),
+                pltpu.SemaphoreType.DMA((5,)),
                 pltpu.SemaphoreType.DMA((6, 2)),
                 pltpu.SemaphoreType.DMA((6, 2)),
+                pltpu.SemaphoreType.REGULAR,
             ],
             compiler_params=pltpu.CompilerParams(
-                has_side_effects=True, vmem_limit_bytes=58 * 1024 * 1024
+                collective_id=0, has_side_effects=True, vmem_limit_bytes=58 * 1024 * 1024
             ),
         )(omega, delta, time, space, inverse)
+        return pl.pallas_call(
+            hand_over,
+            out_shape=(block, block),
+            in_specs=[main] * 2,
+            out_specs=(main, main),
+            scratch_shapes=[pltpu.VMEM(block.shape, jnp.float32), pltpu.VMEM(block.shape, jnp.float32), pltpu.SemaphoreType.DMA((2, PARTS)), pltpu.SemaphoreType.DMA((2, PARTS))],
+            compiler_params=pltpu.CompilerParams(vmem_limit_bytes=60 * 1024 * 1024),
+        )(*results)
 
     specs = (P("tm", "space", None), P("tm", "space", None))
     return jax.shard_map(per_device, mesh=mesh, in_specs=specs, out_specs=specs, check_vma=False)

time: 120 us -> 110 us (0.917)
  Pallas kernels: 115 us -> 110 us
  local copies, waits for them, and re-layouts: 3.74 us -> 0 us
    pallas_call x1 -> x2, Pallas kernels: 115 us -> 110 us  [the longest x1 108 us: per_device(): pl.pallas_call(kernel, out_shape=(block, block), in_specs=[main] * 5, out...]
    unnamed x2 -> x0, local copies, waits for them, and re-layouts: 3.74 us -> none
where the time goes in v2:
time: 110 us
  Pallas kernels  110 us (100%)
    pallas_call x1, Pallas kernels, per_device(): pl.pallas_call(kernel, out_shape=(block, block), in_specs=[main] * 5, out...  108 us

profile of v2, /device:TPU:1, one launch (start us, length us, event | category | flops | bytes accessed | tf_op | source)
XLA Modules:
  0.0 110.3 jit_solution(17083331326887787729)
XLA Ops:
  0.6 107.6 %shard_map.68 = (f32[8,64,256]{2,1,0:T(8,128)}, f32[8,64,256]{2,1,0:T(8,128)}) custom-call(f32[8,64,256]{2,1,0:T(8,128)} %omega_hbm.1, f32[8,64,256]{2,1,0:T(8,128)} %delta_hbm.1, bf16[4,512,512]{2,1,0:T(8,128)(2,1)} %constant.6.clone.time_hbm, bf16[12,256,256]{2,1,0:T(8,128)(2,1)} %constant.7.clone.space_hbm, f32[256,256]{1,0:T(8,128)} %constant.8.clone.inverse_hbm), custom_call_target="tpu_custom_call" | custom-call | tf_op jit(solution)/shard_map/pallas_call | solution.py:397
  108.3 2.0 %shard_map.69 = (f32[8,64,256]{2,1,0:T(8,128)}, f32[8,64,256]{2,1,0:T(8,128)}) custom-call(f32[8,64,256]{2,1,0:T(8,128)} %get-tuple-element.4.residual_in, f32[8,64,256]{2,1,0:T(8,128)} %get-tuple-element.5.jvp_in), custom_call_target="tpu_custom_call" | custom-call | tf_op jit(solution)/shard_map/pallas_call | solution.py:431

commit v3 on v2

--- a/solution.py
+++ b/solution.py
@@ -158,21 +158,14 @@
     for load in loads:
         load.start()
 
-    def far_first(step, plane):
-        later = step - plane
-        level = later // (2 * plane)
-        distance = jnp.where(step < plane, 4, (3 - level) * (1 - 2 * (later % 2)))
-        place = jnp.where(step < plane, step, (later % (2 * plane)) // 2)
-        return distance, jnp.where(level < 3, place, later - 6 * plane + 1)
-
     def tm_partner(step):
-        dz, place = far_first(step, 8)
-        return ((z + dz + 8) % 8) * 8 + ((y + place // 2) % 4) * 2 + (x_lo + place) % 2
+        dz, place = 3 * step, step // 8
+        return ((z + dz) % 8) * 8 + ((y + place // 2) % 4) * 2 + (x_lo + place) % 2
 
     def outer_partner(step):
-        dz, place = far_first(step, 16)
+        dz, place = 3 * step, step // 8
         x = (x_hi * 2 + x_lo + place) % 4
-        return ((z + dz + 8) % 8) * 8 + ((y + place // 4) % 4) * 2 + x % 2, x // 2
+        return ((z + dz) % 8) * 8 + ((y + place // 4) % 4) * 2 + x % 2, x // 2
 
     def settle(buffer, sem):
         pltpu.make_async_copy(buffer, buffer, sem).wait()
@@ -180,9 +173,10 @@
     def rows8(index):
         return pl.ds(pl.multiple_of(index * 8, 8), 8)
 
-    def exchange_tm(stage, a, src, dst):
+    def exchange_tm(stage, a, src, dst, first=0, last=64):
         send, recv = send_sem.at[stage, a], recv_sem.at[stage, a]
-        pltpu.make_async_copy(src.at[a, :, rows8(tm)], dst.at[a, :, rows8(tm)], recv).start()
+        if first == 0:
+            pltpu.make_async_copy(src.at[a, :, rows8(tm)], dst.at[a, :, rows8(tm)], recv).start()
 
         def body(step, carry):
             partner = tm_partner(step)
@@ -196,7 +190,7 @@
             ).start()
             return carry
 
-        lax.fori_loop(0, 63, body, 0)
+        lax.fori_loop(max(first, 1), last, body, 0)
 
     def message(index):
         return pl.ds(pl.multiple_of(index * ROWS, ROWS), ROWS)
@@ -217,7 +211,7 @@
             ).start()
             return carry
 
-        lax.fori_loop(0, OUTER - 1, body, 0)
+        lax.fori_loop(1, OUTER, body, 0)
 
     def span(index):
         return pl.ds(pl.multiple_of(index * SPAN, SPAN), SPAN)
@@ -263,9 +257,11 @@
     pl.semaphore_wait(barrier, len(greeted))
     for device in column:
         pl.semaphore_signal(plane_sem, inc=1, device_id=device, device_id_type=MESH)
+    for a in range(2):
+        exchange_tm(0, a, a_src, a_dst, 0, 8)
     pl.semaphore_wait(plane_sem, len(column))
     for a in range(2):
-        exchange_tm(0, a, a_src, a_dst)
+        exchange_tm(0, a, a_src, a_dst, 8, 64)
 
     row = lax.broadcasted_iota(jnp.int32, (64, NY), 0) + space * 64
     col = lax.broadcasted_iota(jnp.int32, (64, NY), 1)
@@ -369,20 +365,16 @@
 PARTS = 2
 
 
-def hand_over(residual_in, jvp_in, residual_ref, jvp_ref, one, two, sem, out_sem):
-    copies, outs = [], []
-    for a, (src, mid, dst) in enumerate(((residual_in, one, residual_ref), (jvp_in, two, jvp_ref))):
+def hand_over(residual_in, jvp_in, residual_ref, jvp_ref, sem):
+    copies = []
+    for a, (src, dst) in enumerate(((residual_in, residual_ref), (jvp_in, jvp_ref))):
         for k in range(PARTS):
             part = pl.ds(k * (8 // PARTS), 8 // PARTS)
-            copies.append(pltpu.make_async_copy(src.at[part], mid.at[part], sem.at[a, k]))
-            outs.append(pltpu.make_async_copy(mid.at[part], dst.at[part], out_sem.at[a, k]))
+            copies.append(pltpu.make_async_copy(src.at[part], dst.at[part], sem.at[a, k]))
     for copy in copies:
         copy.start()
-    for copy, out in zip(copies, outs):
+    for copy in copies:
         copy.wait()
-        out.start()
-    for out in outs:
-        out.wait()
 
 
 def solution(mesh):
@@ -391,12 +383,13 @@
     def per_device(omega, delta):
         block = jax.ShapeDtypeStruct(omega.shape, jnp.float32)
         vmem, main = pl.BlockSpec(memory_space=pltpu.VMEM), pl.BlockSpec(memory_space=pltpu.HBM)
+        held = pltpu.VMEM(omega.shape, jnp.float32)
         strips = pltpu.VMEM((2, 2, NT, 128), jnp.float32)
         pieces = pltpu.VMEM((2, GROUP, 2, SPAN, 128), jnp.float32)
         tiles = pltpu.VMEM((2, OUTER * ROWS, 128), jnp.float32)
         results = pl.pallas_call(
             kernel,
-            out_shape=(block, block),
+            out_shape=(held, held),
             in_specs=[main] * 5,
             out_specs=(vmem, vmem),
             scratch_shapes=[
@@ -431,11 +424,10 @@
         return pl.pallas_call(
             hand_over,
             out_shape=(block, block),
-            in_specs=[main] * 2,
+            in_specs=[vmem] * 2,
             out_specs=(main, main),
-            scratch_shapes=[pltpu.VMEM(block.shape, jnp.float32), pltpu.VMEM(block.shape, jnp.float32), pltpu.SemaphoreType.DMA((2, PARTS)), pltpu.SemaphoreType.DMA((2, PARTS))],
-            compiler_params=pltpu.CompilerParams(vmem_limit_bytes=60 * 1024 * 1024),
-        )(*results)
+            scratch_shapes=[pltpu.SemaphoreType.DMA((2, PARTS))],
+        )(*[pltpu.with_memory_space_constraint(result, pltpu.VMEM) for result in results])
 
     specs = (P("tm", "space", None), P("tm", "space", None))
     return jax.shard_map(per_device, mesh=mesh, in_specs=specs, out_specs=specs, check_vma=False)

time: 110 us -> 105 us (0.955)
  Pallas kernels: 110 us -> 104 us
    pallas_call x2, Pallas kernels: 110 us -> 104 us  [the longest x1 103 us: per_device(): pl.pallas_call(kernel, out_shape=(held, held), in_specs=[main] * 5, out_s...]
where the time goes in v3:
time: 105 us
  Pallas kernels  104 us (99%)
    pallas_call x1, Pallas kernels, per_device(): pl.pallas_call(kernel, out_shape=(held, held), in_specs=[main] * 5, out_s...  103 us

profile of v3, /device:TPU:1, one launch (start us, length us, event | category | flops | bytes accessed | tf_op | source)
XLA Modules:
  0.0 105.0 jit_solution(16088542280826570081)
XLA Ops:
  0.6 103.4 %shard_map.68 = (f32[8,64,256]{2,1,0:T(8,128)S(1)}, f32[8,64,256]{2,1,0:T(8,128)S(1)}) custom-call(f32[8,64,256]{2,1,0:T(8,128)} %omega_hbm.1, f32[8,64,256]{2,1,0:T(8,128)} %delta_hbm.1, bf16[4,512,512]{2,1,0:T(8,128)(2,1)} %constant.6.clone.time_hbm, bf16[12,256,256]{2,1,0:T(8,128)(2,1)} %constant.7.clone.space_hbm, f32[256,256]{1,0:T(8,128)} %constant.8.clone.inverse_hbm), custom_call_target="tpu_custom_call" | custom-call | tf_op jit(solution)/shard_map/pallas_call | solution.py:390
  104.0 1.0 shard_map.69

commit v4 on v3

--- a/solution.py
+++ b/solution.py
@@ -146,13 +146,14 @@
     ]
 
     barrier = pltpu.get_barrier_semaphore()
-    column = [(((z + dz) % 8) * 8 + y * 2 + x_lo, space) for dz in range(1, 8)]
-    greeted = column + [(tm, x_hi * 2 + (1 - core))]
-    for dy in range(4):
-        for dx in range(4):
+    column = [(((z + dz) % 8) * 8 + y * 2 + x_lo, space) for dz in (4, 3, 5, 2, 6, 1, 7)]
+    greeted = []
+    for dy in (2, 1, 3, 0):
+        for dx in (2, 1, 3, 0):
             if dy or dx:
                 x = (x_hi * 2 + x_lo + dx) % 4
                 greeted.append((z * 8 + ((y + dy) % 4) * 2 + x % 2, (x // 2) * 2 + core))
+    greeted = greeted[:1] + column[:3] + greeted[1:] + column[3:] + [(tm, x_hi * 2 + (1 - core))]
     for device in greeted:
         pl.semaphore_signal(barrier, inc=1, device_id=device, device_id_type=MESH)
     for load in loads:
@@ -162,6 +163,10 @@
         dz, place = 3 * step, step // 8
         return ((z + dz) % 8) * 8 + ((y + place // 2) % 4) * 2 + (x_lo + place) % 2
 
+    def by_plane(step):
+        plane, place = step // 8, step % 8
+        return plane * 8 + ((y + place // 2) % 4) * 2 + (x_lo + place) % 2
+
     def outer_partner(step):
         dz, place = 3 * step, step // 8
         x = (x_hi * 2 + x_lo + place) % 4
@@ -173,24 +178,31 @@
     def rows8(index):
         return pl.ds(pl.multiple_of(index * 8, 8), 8)
 
-    def exchange_tm(stage, a, src, dst, first=0, last=64):
+    def exchange_tm(stage, a, src, dst, first=0, last=64, order=None):
         send, recv = send_sem.at[stage, a], recv_sem.at[stage, a]
         if first == 0:
             pltpu.make_async_copy(src.at[a, :, rows8(tm)], dst.at[a, :, rows8(tm)], recv).start()
 
         def body(step, carry):
-            partner = tm_partner(step)
-            pltpu.make_async_remote_copy(
-                src_ref=src.at[a, :, rows8(partner)],
-                dst_ref=dst.at[a, :, rows8(tm)],
-                send_sem=send,
-                recv_sem=recv,
-                device_id=(partner, space),
-                device_id_type=MESH,
-            ).start()
+            partner = (order or tm_partner)(step)
+
+            def send_one():
+                pltpu.make_async_remote_copy(
+                    src_ref=src.at[a, :, rows8(partner)],
+                    dst_ref=dst.at[a, :, rows8(tm)],
+                    send_sem=send,
+                    recv_sem=recv,
+                    device_id=(partner, space),
+                    device_id_type=MESH,
+                ).start()
+
+            if order is None:
+                send_one()
+            else:
+                pl.when(partner != tm)(send_one)
             return carry
 
-        lax.fori_loop(max(first, 1), last, body, 0)
+        lax.fori_loop(first if order else max(first, 1), last, body, 0)
 
     def message(index):
         return pl.ds(pl.multiple_of(index * ROWS, ROWS), ROWS)
@@ -343,7 +355,7 @@
         value = time_transform(2, both(r1_dst, a))
         for h in range(2):
             b_src[a, h] = value[:, h * 128 : h * 128 + 128]
-        exchange_tm(5, a, b_src, b_dst)
+        exchange_tm(5, a, b_src, b_dst, order=by_plane)
 
     outputs = (residual_ref, jvp_ref)
     for a in range(2):

time: 105 us -> 104 us (level)
  the two profiles are of different devices: /device:TPU:1 before, /device:TPU:64 now
where the time goes in v4:
time: 104 us
  Pallas kernels  103 us (99%)
    pallas_call x1, Pallas kernels, per_device(): pl.pallas_call(kernel, out_shape=(held, held), in_specs=[main] * 5, out_s...  102 us

profile of v4, /device:TPU:64, one launch (start us, length us, event | category | flops | bytes accessed | tf_op | source)
XLA Modules:
  0.0 104.1 jit_solution(15565485267176767028)
XLA Ops:
  0.6 102.4 %shard_map.68 = (f32[8,64,256]{2,1,0:T(8,128)S(1)}, f32[8,64,256]{2,1,0:T(8,128)S(1)}) custom-call(f32[8,64,256]{2,1,0:T(8,128)} %omega_hbm.1, f32[8,64,256]{2,1,0:T(8,128)} %delta_hbm.1, bf16[4,512,512]{2,1,0:T(8,128)(2,1)} %constant.6.clone.time_hbm, bf16[12,256,256]{2,1,0:T(8,128)(2,1)} %constant.7.clone.space_hbm, f32[256,256]{1,0:T(8,128)} %constant.8.clone.inverse_hbm), custom_call_target="tpu_custom_call" | custom-call | tf_op jit(solution)/shard_map/pallas_call | solution.py:402
  103.1 1.0 shard_map.69
